TPU v7x, 512 devices: a whole 4x4x16 slice. The times are simulated.
512 devices in a mesh: group: 8 (over z_lo), member: 64 (over x, y, z_hi, core).
Axes of the slice: x: 4, y: 4, z: 16 (z_hi: 2, z_lo: 8; z = z_hi * 8 + z_lo), core: 2. Of those that a mesh axis runs over, the one named last changes fastest.
Arguments:
- embeddings: bfloat16 [262144, 1024], P(('group', 'member')), may hold values from -6 to 6
- assign: int32 [262144], P(('group', 'member')), may hold values from 0 to 255, as said below
- cluster_list: int32 [512, 64], P(('group', 'member')), may hold values from 0 to 255, as said below
- owner_map: int32 [8, 256], P('group'), may hold values from 0 to 255, as said below
- old_centroids: float32 [2048, 1024], P(('group', 'member')), may hold values from -16 to 16
Outputs:
- centroids: bfloat16 [2048, 1024], P(('group', 'member'))
- block_max: float32 [262144, 512], P(('group', 'member'))
Inputs may be any that keep to these rules, and one draw needn't show every extreme that they name: Each row of owner_map is a permutation; the centroid at position p of group g is row g * 256 + p of old_centroids and centroids. `cluster_list`: each device lists 64 distinct clusters of its group's slab. Of the 4 clusters whose positions p share p // 4, a device lists at most 2, and every device lists exactly 2 of some such set. `assign`: A cluster number within the slab of the row's group.
All inputs are finite; a program needn't handle non-finite values.
Results may differ from a plain program's by a relative error of at most 0.0023.
Values may be sent and summed in bfloat16 or wider, within the bound.
A program may use at most 64 MiB of HBM per device.

v0:
```python
import math
import jax
import jax.numpy as jnp
from jax import lax
from jax.sharding import PartitionSpec as P


def shards(embeddings, assign, cluster_list, owner_map, old_centroids):
    per_owner = old_centroids.shape[0]
    slab_rows = owner_map.shape[1]
    width = embeddings.shape[1]
    listed_ids = cluster_list[0]
    owner_row = owner_map[0]
    lookup = listed_ids[:, None] == jnp.arange(slab_rows, dtype=jnp.int32)[None, :]
    listed_pos = jnp.sum(jnp.where(lookup, owner_row[None, :], 0), axis=1)
    matched = assign[:, None] == listed_ids[None, :]
    row_target = jnp.sum(jnp.where(matched, listed_pos[None, :] + 1, 0), axis=1) - 1
    one_hot = (row_target[None, :] == jnp.arange(slab_rows, dtype=jnp.int32)[:, None]).astype(
        jnp.bfloat16
    )
    partial_value = jnp.dot(one_hot, embeddings, preferred_element_type=jnp.float32)
    tallies = jnp.sum(one_hot.astype(jnp.float32), axis=1)
    cluster_sums, counts = (
        lax.psum_scatter(partial_value, "member", scatter_dimension=0, tiled=True),
        lax.psum_scatter(tallies, "member", scatter_dimension=0, tiled=True),
    )
    updated = (cluster_sums + old_centroids) / (counts + 1.0)[:, None]
    centroids = (
        updated * lax.rsqrt(jnp.mean(updated * updated, axis=1, keepdims=True) + 1e-05)
    ).astype(jnp.bfloat16)
    inverse_root = 1.0 / math.sqrt(width)
    whole_slab = lax.all_gather(centroids, "member", axis=0, tiled=True)
    shard_rows = lax.all_gather(whole_slab, "group", axis=0, tiled=True)
    similarity = (
        lax.dot_general(
            embeddings, shard_rows, (((1,), (1,)), ((), ())), preferred_element_type=jnp.float32
        )
        * inverse_root
    )
    blocks = jnp.max(
        similarity.reshape(similarity.shape[0], shard_rows.shape[0] // per_owner, per_owner), axis=2
    )
    return (centroids, blocks)


def solution(mesh):
    in_specs = (
        P(("group", "member"), None),
        P(("group", "member")),
        P(("group", "member"), None),
        P("group", None),
        P(("group", "member"), None),
    )
    out_specs = (P(("group", "member"), None), P(("group", "member"), None))
    return jax.shard_map(shards, mesh=mesh, in_specs=in_specs, out_specs=out_specs, check_vma=False)
```

profile of v0, /device:TPU:1, one launch (start us, length us, event | category | flops | bytes accessed | tf_op | source)
XLA Modules:
  0.0 1374.8 jit_solution(14540987311990371259)
XLA Ops:
  7.2 0.0 copy-start
  7.2 0.0 all-reduce.4.cloned.1.call-start
  7.2 0.9 select_reduce_fusion.1
  8.2 0.8 select_reduce_fusion
  9.0 0.0 copy-done
  9.0 1.4 fusion.1
  10.4 0.0 all-reduce.4.cloned.1.call-update
  10.4 0.0 all-gather.3.cloned.1.call-start
  10.5 1.3 dynamic-slice
  12.4 0.1 convert_reduce_fusion
  12.5 284.2 %all-reduce.1 = f32[256]{0:T(256)S(1)} all-reduce(f32[256]{0:T(256)S(1)} %convert_reduce_fusion), channel_id=3, replica_groups=mesh['group'=8,'member'=64] {'member'}, use_global_device_ids=true, to_apply=%region_4.5.clone | all-reduce | flops 256 | bytes 2048
  296.7 0.1 dynamic-slice_add_fusion.1
  296.8 797.9 %all-reduce.4.cloned.1.call-done = f32[256,1024]{1,0:T(8,128)} async-done(((f32[256,1024]{1,0:T(8,128)}), f32[256,1024]{1,0:T(8,128)}) %all-reduce.4.cloned.1.call-update) | async-done | bytes 1048592
  1094.7 1.0 multiply_reduce_fusion
  1095.6 0.1 fusion.8
  1095.7 161.9 %all-gather = bf16[64,4,1024]{2,1,0:T(4,128)(2,1)S(1)} all-gather(bf16[1,4,1024]{2,1,0:T(4,128)(2,1)S(1)} %fusion.8), channel_id=1, replica_groups=mesh['group'=8,'member'=64] {'member'}, dimensions={0}, use_global_device_ids=true | all-gather | bytes 532480 | tf_op jit(solution)/shard_map/all_gather | solution.py:32
  1257.6 0.9 reshape.27
  1258.6 0.0 all-gather.3.cloned.1.call-update
  1258.6 0.7 multiply_convert_fusion
  1259.3 91.1 %all-gather.3.cloned.1.call-done = bf16[2048,1024]{1,0:T(8,128)(2,1)} async-done(((bf16[256,1024]{1,0:T(8,128)(2,1)}), bf16[2048,1024]{1,0:T(8,128)(2,1)}) %all-gather.3.cloned.1.call-update) | async-done | bytes 4194320 | tf_op jit(solution)/shard_map/all_gather | solution.py:33
  1350.3 6.5 multiply_bitcast_fusion
  1356.8 5.2 reshape.25
  1362.0 4.7 reduce_max.9
  1366.7 1.3 copy.8
  (3 shorter events, 0.0 us)
Async XLA Ops:
  7.2 1.8 copy-start
  7.2 1087.5 %all-reduce.4.cloned.1.call-start = ((), (), s32[]{:S(2)}) async-start(), calls=%async_computation.1 | async-start | bytes 2097152
  10.4 1339.9 %all-gather.3.cloned.1.call-start = ((), (), s32[]{:S(2)}) async-start(), calls=%async_computation | async-start | bytes 4718592 | tf_op jit(solution)/shard_map/all_gather | solution.py:33
Sparse Core Ops, SparseCore 0:
  11.5 1083.1 all-reduce.3
  1258.7 91.5 all-gather.2
where the time goes:
time: 1380 us; the launch traced here: 1370 us
  waiting for transfers between devices  889 us (64%)
  blocking collectives  446 us (32%)
  between operations  14.7 us (1%)
    unnamed x3, waiting for transfers between devices  798 us
    unnamed x1, blocking collectives  284 us
    all_gather x1, blocking collectives, shards(): whole_slab = lax.all_gather(centroids, 'member', axis=0, tiled=True)  162 us
    all_gather x1, waiting for transfers between devices, shards(): shard_rows = lax.all_gather(whole_slab, 'group', axis=0, tiled=True)  91.1 us
  transfers between devices with their start and end apart: 2, of which 2 were waited for; matrix products, arithmetic and copies ran while one was open for 0% of the time, Pallas kernels for 0%

commit v1 on v0

--- a/solution.py
+++ b/solution.py
@@ -29,7 +29,9 @@
         updated * lax.rsqrt(jnp.mean(updated * updated, axis=1, keepdims=True) + 1e-05)
     ).astype(jnp.bfloat16)
     inverse_root = 1.0 / math.sqrt(width)
-    whole_slab = lax.all_gather(centroids, "member", axis=0, tiled=True)
+    whole_slab = jnp.concatenate(
+        lax.all_to_all(jnp.stack([centroids] * lax.axis_size("member")), "member", 0, 0), axis=0
+    )
     shard_rows = lax.all_gather(whole_slab, "group", axis=0, tiled=True)
     similarity = (
         lax.dot_general(

time: 1380 us -> 1270 us (0.920)
  blocking collectives: 446 us -> 330 us
    all_gather x1 -> x0, blocking collectives: 162 us -> none  [shards(): whole_slab = lax.all_gather(centroids, 'member', axis=0, tiled=True)]
    all_to_all x0 -> x1, blocking collectives: none -> 45.6 us  [shards(): lax.all_to_all(jnp.stack([centroids] * lax.axis_size('member')), 'member'...]
where the time goes in v1:
time: 1270 us
  waiting for transfers between devices  898 us (71%)
  blocking collectives  330 us (26%)
  between operations  14.7 us (1%)
    unnamed x3, waiting for transfers between devices  798 us
    unnamed x1, blocking collectives  284 us
    all_gather x1, waiting for transfers between devices, shards(): shard_rows = lax.all_gather(whole_slab, 'group', axis=0, tiled=True)  101 us
    all_to_all x1, blocking collectives, shards(): lax.all_to_all(jnp.stack([centroids] * lax.axis_size('member')), 'member'...  45.6 us
  transfers between devices with their start and end apart: 2, of which 2 were waited for; matrix products, arithmetic and copies ran while one was open for 0% of the time, Pallas kernels for 0%

profile of v1, /device:TPU:1, one launch (start us, length us, event | category | flops | bytes accessed | tf_op | source)
XLA Modules:
  0.0 1267.4 jit_solution(13326041463018158591)
XLA Ops:
  7.2 0.0 copy-start
  7.2 0.0 all-reduce.4.cloned.1.call-start
  7.2 0.9 select_reduce_fusion.1
  8.2 0.8 select_reduce_fusion
  9.0 0.0 copy-done
  9.0 1.4 fusion.1
  10.4 0.0 all-reduce.4.cloned.1.call-update
  10.4 0.0 all-gather.2.cloned.1.call-start
  10.5 1.3 dynamic-slice
  12.4 0.1 convert_reduce_fusion
  12.5 284.2 %all-reduce.1 = f32[256]{0:T(256)S(1)} all-reduce(f32[256]{0:T(256)S(1)} %convert_reduce_fusion), channel_id=3, replica_groups=mesh['group'=8,'member'=64] {'member'}, use_global_device_ids=true, to_apply=%region_4.5.clone | all-reduce | flops 256 | bytes 2048
  296.7 0.1 dynamic-slice_add_fusion.1
  296.8 797.9 %all-reduce.4.cloned.1.call-done = f32[256,1024]{1,0:T(8,128)} async-done(((f32[256,1024]{1,0:T(8,128)}), f32[256,1024]{1,0:T(8,128)}) %all-reduce.4.cloned.1.call-update) | async-done | bytes 1048592
  1094.7 1.0 multiply_reduce_fusion
  1095.6 0.1 multiply_convert_fusion
  1095.7 0.0 copy-start.1
  1095.7 0.1 stack.2
  1095.9 45.6 %all_to_all.5 = bf16[64,4,1024]{2,1,0:T(4,128)(2,1)S(1)} all-to-all(bf16[64,4,1024]{2,1,0:T(4,128)(2,1)S(1)} %stack.2), channel_id=1, replica_groups=mesh['group'=8,'member'=64] {'member'}, dimensions={0} | all-to-all | bytes 1048576 | tf_op jit(solution)/shard_map/all_to_all | solution.py:33
  1141.4 0.9 reshape.30
  1142.4 0.0 all-gather.2.cloned.1.call-update
  1142.4 100.5 %all-gather.2.cloned.1.call-done = bf16[2048,1024]{1,0:T(8,128)(2,1)} async-done(((bf16[256,1024]{1,0:T(8,128)(2,1)}), bf16[2048,1024]{1,0:T(8,128)(2,1)}) %all-gather.2.cloned.1.call-update) | async-done | bytes 4194320 | tf_op jit(solution)/shard_map/all_gather | solution.py:35
  1242.9 6.5 multiply_bitcast_fusion
  1249.4 0.0 copy-done.1
  1249.4 5.2 reshape.31
  1254.6 4.7 reduce_max.9
  1259.3 1.3 copy.8
  (3 shorter events, 0.0 us)
Async XLA Ops:
  7.2 1.8 copy-start
  7.2 1087.5 %all-reduce.4.cloned.1.call-start = ((), (), s32[]{:S(2)}) async-start(), calls=%async_computation.2 | async-start | bytes 2097152
  10.4 1232.5 %all-gather.2.cloned.1.call-start = ((), (), s32[]{:S(2)}) async-start(), calls=%async_computation.1 | async-start | bytes 4718592 | tf_op jit(solution)/shard_map/all_gather | solution.py:35
  1095.7 153.7 %copy-start.1 = (bf16[4,1024]{1,0:T(4,128)(2,1)}, bf16[4,1024]{1,0:T(4,128)(2,1)S(1)}, u32[]{:S(2)}) copy-start(bf16[4,1024]{1,0:T(4,128)(2,1)S(1)} %multiply_convert_fusion) | copy-start | bytes 24580
Sparse Core Ops, SparseCore 0:
  11.5 1083.1 all-reduce.3
  1142.5 100.3 all-gather.1
